TPU v7x, 512 devices: a whole 4x4x16 slice. The times are simulated.
512 devices in a mesh: blk: 32 (over z, core), grp: 16 (over y, x).
Axes of the slice: x: 4, y: 4, z: 16, core: 2. Of those that a mesh axis runs over, the one named last changes fastest.
Arguments:
- labels: float32 [16, 16384, 256], P('grp', 'blk'), may hold values from 0.1 to 10
- tiles: bfloat16 [16, 128, 16, 128, 128], P('grp', 'blk'), may hold values from 0.001 to 1
- tile_cols: int32 [16, 128, 16], P('grp', 'blk'), may hold values from 0 to 23
- tile_count: int32 [16, 128], P('grp', 'blk'), may hold values from 4 to 16
- send_blocks: int32 [16, 32, 16, 1], P('grp', 'blk'), may hold values from 0 to 3
Outputs:
- spread: float32 [16, 16384, 256], P('grp', 'blk')
All inputs are finite; a program needn't handle non-finite values.
Results may differ from a plain program's by a relative error of at most 0.0006.
Values may be sent and summed in bfloat16 or wider, within the bound.
A program may use at most 64 MiB of HBM per device.

v0:
```python
import jax
import jax.numpy as jnp
from jax import lax
from jax.sharding import PartitionSpec as P

HB = 2
ITERS = 3


def with_halo(block, sides, width):
    for axis, dim in sides:
        count = lax.axis_size(axis)
        forward = [(i, i + 1) for i in range(count - 1)]
        backward = [(target, source) for source, target in forward]
        low = lax.ppermute(
            lax.slice_in_dim(block, block.shape[dim] - width, None, axis=dim), axis, forward
        )
        high = lax.ppermute(lax.slice_in_dim(block, 0, width, axis=dim), axis, backward)
        block = jnp.concatenate([low, block, high], axis=dim)
    return block


def on_device(labels, tiles, tile_cols, tile_count, send_blocks):
    n_rows = tiles.shape[1]
    kmax = tiles.shape[2]
    bsize = tiles.shape[3]
    classes = labels.shape[2]
    n_bands = lax.axis_size("grp")
    slots = jnp.arange(kmax, dtype=jnp.int32)
    valid = slots[None, :] < tile_count[0][:, None]
    row_sums = jnp.sum(tiles[0], axis=-1, dtype=jnp.float32)
    deg = jnp.sum(jnp.where(valid[..., None], row_sums, 0.0), axis=1)
    scale = lax.rsqrt(deg).reshape(n_rows * bsize)
    anchor = labels[0]
    picks = send_blocks[0, 0]
    band_ids = jnp.arange(n_bands, dtype=jnp.int32)
    arrived = lax.all_to_all(picks, "grp", split_axis=0, concat_axis=0, tiled=True)
    field = anchor
    for step in range(ITERS):
        scaled = (scale[:, None] * field).astype(jnp.bfloat16)
        padded = with_halo(scaled, (("blk", 0),), HB * bsize)
        local = padded.reshape(n_rows + 2 * HB, bsize, classes)
        own_blocks = scaled.reshape(n_rows, bsize, classes)
        copies = lax.all_gather(own_blocks[None], "grp", axis=0, tiled=True)
        cross = copies[band_ids[:, None], arrived]
        ext = jnp.concatenate([local, cross.reshape(-1, bsize, classes)], axis=0)
        chosen = jnp.where(valid[..., None, None], ext[tile_cols[0]], jnp.zeros((), jnp.bfloat16))
        summed = jnp.einsum("rkij,rkjc->ric", tiles[0], chosen, preferred_element_type=jnp.float32)
        summed = summed.reshape(n_rows * bsize, classes)
        update = 0.9 * scale[:, None] * summed + 0.1 * anchor
        field = update / jnp.mean(update, axis=-1, keepdims=True)
    return field[None]


def solution(mesh):
    return jax.shard_map(
        on_device,
        mesh=mesh,
        in_specs=(
            P("grp", "blk", None),
            P("grp", "blk", None, None, None),
            P("grp", "blk", None),
            P("grp", "blk"),
            P("grp", "blk", None, None),
        ),
        out_specs=P("grp", "blk", None),
        check_vma=False,
    )
```

profile of v0, /device:TPU:1, one launch (start us, length us, event | category | flops | bytes accessed | tf_op | source)
XLA Modules:
  0.0 261.9 jit_solution(1155358600882321074)
XLA Ops:
  6.5 0.0 all-gather.6.cloned.1.call-start
  6.5 0.8 iota_compare_fusion
  7.3 2.2 convert_reduce_fusion
  9.6 0.1 select_reduce_fusion
  9.7 1.9 multiply_convert_fusion.2
  11.5 0.0 all-gather.6.cloned.1.call-update
  11.6 1.3 copy.10
  12.9 7.6 %all-to-all-start = ((s32[16,1,1]{2,1,0:T(1,128)}), s32[16,1,1]{2,1,0:T(1,128)S(1)}, u32[]{:S(2)}, u32[]{:S(2)}) async-start(s32[16,1,1]{2,1,0:T(1,128)} %copy.10), calls=%async_computation | async-start | bytes 16384 | tf_op jit(solution)/shard_map/all_to_all | solution.py:37
  20.5 0.0 all-gather.8.cloned.1.call-start
  20.5 1.2 fusion.25
  21.7 4.4 %collective-permute-start = (bf16[256,256]{1,0:T(8,128)(2,1)S(1)}, bf16[256,256]{1,0:T(8,128)(2,1)S(1)}, u32[]{:S(2)}, u32[]{:S(2)}) collective-permute-start(bf16[256,256]{1,0:T(8,128)(2,1)S(1)} %get-tuple-element.9), channel_id=1, source_target_pairs={{0,16},{16,32},{32,48},{48,64},{64,80},{80,96},{96,112},{112,128},... | collective-permute-start | bytes 393224 | tf_op jit(solution)/shard_map/ppermute | solution.py:15
  26.1 1.9 collective-permute-start.1
  28.1 0.1 reshape.310
  28.2 0.0 all-to-all-done
  28.3 0.1 copy.11
  28.4 0.0 collective-permute-done
  28.4 4.0 %collective-permute-done.1 = bf16[256,256]{1,0:T(8,128)(2,1)S(1)} collective-permute-done((bf16[256,256]{1,0:T(8,128)(2,1)S(1)}, bf16[256,256]{1,0:T(8,128)(2,1)S(1)}, u32[]{:S(2)}, u32[]{:S(2)}) %collective-permute-start.1) | collective-permute-done | bytes 131104 | tf_op jit(solution)/shard_map/ppermute | solution.py:18
  32.5 51.4 %all-gather.6.cloned.1.call-done = bf16[16,4,128,256]{3,2,1,0:T(8,128)(2,1)} async-done(((bf16[1,4,128,256]{3,2,1,0:T(8,128)(2,1)}), bf16[16,4,128,256]{3,2,1,0:T(8,128)(2,1)}) %all-gather.6.cloned.1.call-update) | async-done | bytes 4194320 | tf_op jit(solution)/shard_map/all_gather | solution.py:44
  83.9 3.8 %gather_fusion = bf16[16,128,256]{2,1,0:T(8,128)(2,1)} fusion(bf16[16,4,128,256]{3,2,1,0:T(8,128)(2,1)} %all-gather.6.cloned.1.call-done, s32[16]{0:T(128)S(1)} %or_bitcast_fusion), kind=kCustom, calls=%fused_computation | custom fusion | bytes 2097280 | tf_op jit(solution)/shard_map/gather | solution.py:45
  87.6 1.4 pad_maximum_fusion
  89.0 2.8 %gather_fusion.1 = bf16[64,128,256]{2,1,0:T(8,128)(2,1)} fusion(bf16[24,128,256]{2,1,0:T(8,128)(2,1)S(1)} %pad_maximum_fusion, s32[1024]{0:T(1024)S(1)} %pad_clamp_fusion), kind=kCustom, calls=%fused_computation.1 | custom fusion | bytes 8388864 | tf_op jit(solution)/shard_map/gather | solution.py:47
  91.8 3.8 %fusion.28 = (f32[4,128]{1,0:T(4,128)S(1)}, f32[4,256,128,1]{1,2,3,0:T(8,128)S(1)}) fusion(f32[4,128,256]{2,1,0:T(8,128)S(1)} %bitcast.108, f32[4,128]{1,0:T(4,128)S(1)} %get-tuple-element.15, bf16[4,16,128,256]{3,2,1,0:T(8,128)(2,1)} %bitcast.114, pred[4,16]{1,0:T(4,128)(4,1)S(1)} %iota_compare_fusion, bf16[1,4,16,128,128]{4,3,2,1,0:T(8,128)(2,1)} %param.6), kind=kOutput, calls=%fused_computation.53 | convolution fusion | flops 539360768 | bytes 7344192 | tf_op jit(solution)/shard_map/rkij,rkjc->ric/dot_general | solution.py:48
  95.5 1.0 multiply_convert_fusion.1
  96.5 0.0 all-gather.8.cloned.1.call-update
  96.5 0.0 all-gather.10.cloned.1.call-start
  96.6 0.3 fusion.26
  96.9 3.7 %collective-permute-start.2 = (bf16[256,256]{1,0:T(8,128)(2,1)S(1)}, bf16[256,256]{1,0:T(8,128)(2,1)S(1)}, u32[]{:S(2)}, u32[]{:S(2)}) collective-permute-start(bf16[256,256]{1,0:T(8,128)(2,1)S(1)} %get-tuple-element.7), channel_id=1, source_target_pairs={{0,16},{16,32},{32,48},{48,64},{64,80},{80,96},{96,112},{112,128},... | collective-permute-start | bytes 393224 | tf_op jit(solution)/shard_map/ppermute | solution.py:15
  100.6 1.9 collective-permute-start.3
  102.6 0.0 collective-permute-done.2
  102.6 4.3 %collective-permute-done.3 = bf16[256,256]{1,0:T(8,128)(2,1)S(1)} collective-permute-done((bf16[256,256]{1,0:T(8,128)(2,1)S(1)}, bf16[256,256]{1,0:T(8,128)(2,1)S(1)}, u32[]{:S(2)}, u32[]{:S(2)}) %collective-permute-start.3) | collective-permute-done | bytes 131104 | tf_op jit(solution)/shard_map/ppermute | solution.py:18
  107.0 56.3 %all-gather.8.cloned.1.call-done = bf16[64,128,256]{2,1,0:T(8,128)(2,1)} async-done(((bf16[4,128,256]{2,1,0:T(8,128)(2,1)}), bf16[64,128,256]{2,1,0:T(8,128)(2,1)}) %all-gather.8.cloned.1.call-update) | async-done | bytes 4194320 | tf_op jit(solution)/shard_map/all_gather | solution.py:44
  163.3 3.8 %gather_fusion.2 = bf16[16,128,256]{2,1,0:T(8,128)(2,1)} fusion(bf16[16,4,128,256]{3,2,1,0:T(8,128)(2,1)} %bitcast.120, s32[16]{0:T(128)S(1)} %or_bitcast_fusion), kind=kCustom, calls=%fused_computation.2 | custom fusion | bytes 2097280 | tf_op jit(solution)/shard_map/gather | solution.py:45
  167.1 1.4 pad_maximum_fusion.1
  168.4 2.8 %gather_fusion.3 = bf16[64,128,256]{2,1,0:T(8,128)(2,1)} fusion(bf16[24,128,256]{2,1,0:T(8,128)(2,1)S(1)} %pad_maximum_fusion.1, s32[1024]{0:T(1024)S(1)} %pad_clamp_fusion), kind=kCustom, calls=%fused_computation.3 | custom fusion | bytes 8388864 | tf_op jit(solution)/shard_map/gather | solution.py:47
  171.2 3.8 %fusion.29 = (f32[4,128]{1,0:T(4,128)S(1)}, f32[4,256,128,1]{1,2,3,0:T(8,128)S(1)}) fusion(f32[4,128,256]{2,1,0:T(8,128)S(1)} %bitcast.110, f32[4,128]{1,0:T(4,128)S(1)} %get-tuple-element.15, bf16[4,16,128,256]{3,2,1,0:T(8,128)(2,1)} %bitcast.115, pred[4,16]{1,0:T(4,128)(4,1)S(1)} %iota_compare_fusion, bf16[1,4,16,128,128]{4,3,2,1,0:T(8,128)(2,1)} %param.6), kind=kOutput, calls=%fused_computation.54 | convolution fusion | flops 539360768 | bytes 7344192 | tf_op jit(solution)/shard_map/rkij,rkjc->ric/dot_general | solution.py:48
  175.0 1.0 multiply_convert_fusion
  176.0 0.0 all-gather.10.cloned.1.call-update
  176.0 0.3 fusion.27
  176.3 3.7 %collective-permute-start.4 = (bf16[256,256]{1,0:T(8,128)(2,1)S(1)}, bf16[256,256]{1,0:T(8,128)(2,1)S(1)}, u32[]{:S(2)}, u32[]{:S(2)}) collective-permute-start(bf16[256,256]{1,0:T(8,128)(2,1)S(1)} %get-tuple-element.5), channel_id=1, source_target_pairs={{0,16},{16,32},{32,48},{48,64},{64,80},{80,96},{96,112},{112,128},... | collective-permute-start | bytes 393224 | tf_op jit(solution)/shard_map/ppermute | solution.py:15
  180.0 1.9 collective-permute-start.5
  182.0 0.0 collective-permute-done.4
  182.0 4.3 %collective-permute-done.5 = bf16[256,256]{1,0:T(8,128)(2,1)S(1)} collective-permute-done((bf16[256,256]{1,0:T(8,128)(2,1)S(1)}, bf16[256,256]{1,0:T(8,128)(2,1)S(1)}, u32[]{:S(2)}, u32[]{:S(2)}) %collective-permute-start.5) | collective-permute-done | bytes 131104 | tf_op jit(solution)/shard_map/ppermute | solution.py:18
  186.4 56.4 %all-gather.10.cloned.1.call-done = bf16[64,128,256]{2,1,0:T(8,128)(2,1)} async-done(((bf16[4,128,256]{2,1,0:T(8,128)(2,1)}), bf16[64,128,256]{2,1,0:T(8,128)(2,1)}) %all-gather.10.cloned.1.call-update) | async-done | bytes 4194320 | tf_op jit(solution)/shard_map/all_gather | solution.py:44
  242.8 3.8 %gather_fusion.4 = bf16[16,128,256]{2,1,0:T(8,128)(2,1)} fusion(bf16[16,4,128,256]{3,2,1,0:T(8,128)(2,1)} %bitcast.121, s32[16]{0:T(128)S(1)} %or_bitcast_fusion), kind=kCustom, calls=%fused_computation.4 | custom fusion | bytes 2097280 | tf_op jit(solution)/shard_map/gather | solution.py:45
  246.5 1.4 pad_maximum_fusion.2
  247.9 2.8 %gather_fusion.5 = bf16[64,128,256]{2,1,0:T(8,128)(2,1)} fusion(bf16[24,128,256]{2,1,0:T(8,128)(2,1)S(1)} %pad_maximum_fusion.2, s32[1024]{0:T(1024)S(1)} %pad_clamp_fusion), kind=kCustom, calls=%fused_computation.5 | custom fusion | bytes 8388864 | tf_op jit(solution)/shard_map/gather | solution.py:47
  250.6 3.7 %fusion.22 = (f32[4,128]{1,0:T(4,128)S(1)}, f32[4,256,128,1]{1,2,3,0:T(8,128)S(1)}) fusion(f32[4,128,256]{2,1,0:T(8,128)S(1)} %bitcast.112, f32[4,128]{1,0:T(4,128)S(1)} %get-tuple-element.15, bf16[4,16,128,256]{3,2,1,0:T(8,128)(2,1)} %bitcast.113, pred[4,16]{1,0:T(4,128)(4,1)S(1)} %iota_compare_fusion, bf16[1,4,16,128,128]{4,3,2,1,0:T(8,128)(2,1)} %param.6), kind=kOutput, calls=%fused_computation.38 | convolution fusion | flops 539360768 | bytes 7344192 | tf_op jit(solution)/shard_map/rkij,rkjc->ric/dot_general | solution.py:48
  254.4 1.0 add_divide_fusion
  (22 shorter events, 0.3 us)
Async XLA Ops:
  6.5 21.6 %copy-start = (f32[1,512,256]{2,1,0:T(8,128)S(1)}, f32[1,512,256]{2,1,0:T(8,128)}, u32[]{:S(2)}) copy-start(f32[1,512,256]{2,1,0:T(8,128)} %param.5) | copy-start | bytes 1572868
  6.5 21.5 %copy-start.1 = (s32[1,4,16]{2,1,0:T(4,128)S(1)}, s32[1,4,16]{2,1,0:T(4,128)}, u32[]{:S(2)}) copy-start(s32[1,4,16]{2,1,0:T(4,128)} %param.7) | copy-start | bytes 772
  6.5 77.3 %all-gather.6.cloned.1.call-start = ((), (), s32[]{:S(2)}) async-start(), calls=%async_computation.1 | async-start | bytes 4456448 | tf_op jit(solution)/shard_map/all_gather | solution.py:44
  12.9 15.4 %all-to-all-start = ((s32[16,1,1]{2,1,0:T(1,128)}), s32[16,1,1]{2,1,0:T(1,128)S(1)}, u32[]{:S(2)}, u32[]{:S(2)}) async-start(s32[16,1,1]{2,1,0:T(1,128)} %copy.10), calls=%async_computation | async-start | bytes 16384 | tf_op jit(solution)/shard_map/all_to_all | solution.py:37
  20.5 142.8 %all-gather.8.cloned.1.call-start = ((), (), s32[]{:S(2)}) async-start(), calls=%async_computation.2 | async-start | bytes 4456448 | tf_op jit(solution)/shard_map/all_gather | solution.py:44
  21.7 6.6 %collective-permute-start = (bf16[256,256]{1,0:T(8,128)(2,1)S(1)}, bf16[256,256]{1,0:T(8,128)(2,1)S(1)}, u32[]{:S(2)}, u32[]{:S(2)}) collective-permute-start(bf16[256,256]{1,0:T(8,128)(2,1)S(1)} %get-tuple-element.9), channel_id=1, source_target_pairs={{0,16},{16,32},{32,48},{48,64},{64,80},{80,96},{96,112},{112,128},... | collective-permute-start | bytes 393224 | tf_op jit(solution)/shard_map/ppermute | solution.py:15
  26.1 6.3 %collective-permute-start.1 = (bf16[256,256]{1,0:T(8,128)(2,1)S(1)}, bf16[256,256]{1,0:T(8,128)(2,1)S(1)}, u32[]{:S(2)}, u32[]{:S(2)}) collective-permute-start(bf16[256,256]{1,0:T(8,128)(2,1)S(1)} %get-tuple-element.10), channel_id=1, source_target_pairs={{16,0},{32,16},{48,32},{64,48},{80,64},{96,80},{112,96},{128,112},... | collective-permute-start | bytes 393224 | tf_op jit(solution)/shard_map/ppermute | solution.py:18
  96.5 146.2 %all-gather.10.cloned.1.call-start = ((), (), s32[]{:S(2)}) async-start(), calls=%async_computation.3 | async-start | bytes 4456448 | tf_op jit(solution)/shard_map/all_gather | solution.py:44
  96.9 5.7 %collective-permute-start.2 = (bf16[256,256]{1,0:T(8,128)(2,1)S(1)}, bf16[256,256]{1,0:T(8,128)(2,1)S(1)}, u32[]{:S(2)}, u32[]{:S(2)}) collective-permute-start(bf16[256,256]{1,0:T(8,128)(2,1)S(1)} %get-tuple-element.7), channel_id=1, source_target_pairs={{0,16},{16,32},{32,48},{48,64},{64,80},{80,96},{96,112},{112,128},... | collective-permute-start | bytes 393224 | tf_op jit(solution)/shard_map/ppermute | solution.py:15
  100.6 6.3 %collective-permute-start.3 = (bf16[256,256]{1,0:T(8,128)(2,1)S(1)}, bf16[256,256]{1,0:T(8,128)(2,1)S(1)}, u32[]{:S(2)}, u32[]{:S(2)}) collective-permute-start(bf16[256,256]{1,0:T(8,128)(2,1)S(1)} %get-tuple-element.8), channel_id=1, source_target_pairs={{16,0},{32,16},{48,32},{64,48},{80,64},{96,80},{112,96},{128,112},... | collective-permute-start | bytes 393224 | tf_op jit(solution)/shard_map/ppermute | solution.py:18
  176.3 5.7 %collective-permute-start.4 = (bf16[256,256]{1,0:T(8,128)(2,1)S(1)}, bf16[256,256]{1,0:T(8,128)(2,1)S(1)}, u32[]{:S(2)}, u32[]{:S(2)}) collective-permute-start(bf16[256,256]{1,0:T(8,128)(2,1)S(1)} %get-tuple-element.5), channel_id=1, source_target_pairs={{0,16},{16,32},{32,48},{48,64},{64,80},{80,96},{96,112},{112,128},... | collective-permute-start | bytes 393224 | tf_op jit(solution)/shard_map/ppermute | solution.py:15
  180.0 6.3 %collective-permute-start.5 = (bf16[256,256]{1,0:T(8,128)(2,1)S(1)}, bf16[256,256]{1,0:T(8,128)(2,1)S(1)}, u32[]{:S(2)}, u32[]{:S(2)}) collective-permute-start(bf16[256,256]{1,0:T(8,128)(2,1)S(1)} %get-tuple-element.6), channel_id=1, source_target_pairs={{16,0},{32,16},{48,32},{64,48},{80,64},{96,80},{112,96},{128,112},... | collective-permute-start | bytes 393224 | tf_op jit(solution)/shard_map/ppermute | solution.py:18
Sparse Core Ops, SparseCore 0:
  11.7 72.1 all-gather.5
  96.6 66.6 all-gather.7
  176.1 66.6 all-gather.9
where the time goes:
time: 263 us; the launch traced here: 262 us
  waiting for transfers between devices  177 us (67%)
  starting transfers between devices  25.3 us (10%)
  local copies, waits for them, and re-layouts  21.1 us (8%)
  other arithmetic  14 us (5%)
  between operations  13.3 us (5%)
  matrix products  11.3 us (4%)
    all_gather x3, waiting for transfers between devices, on_device(): copies = lax.all_gather(own_blocks[None], 'grp', axis=0, tiled=True)  164 us
    ppermute x3, waiting for transfers between devices, with_halo(): lax.ppermute(lax.slice_in_dim(block, 0, width, axis=dim), axis, backward)  12.7 us
    ppermute x3, starting transfers between devices, with_halo(): lax.ppermute(lax.slice_in_dim(block, block.shape[dim] - width, None, axis...  11.9 us
    gather x3, local copies, waits for them, and re-layouts, on_device(): cross = copies[band_ids[:, None], arrived]  11.3 us
    dot_general x3, matrix products, on_device(): jnp.einsum('rkij,rkjc->ric', tiles[0], chosen, preferred_element_type=jnp...  11.3 us
    gather x3, local copies, waits for them, and re-layouts, on_device(): ext[tile_cols[0]]  8.28 us
    all_to_all x1, starting transfers between devices, on_device(): lax.all_to_all(picks, 'grp', split_axis=0, concat_axis=0, tiled=True)  7.58 us
    ppermute x3, starting transfers between devices, with_halo(): lax.ppermute(lax.slice_in_dim(block, 0, width, axis=dim), axis, backward)  5.76 us
  transfers between devices with their start and end apart: 10, of which 6 were waited for; matrix products, arithmetic and copies ran while one was open for 1% of the time, Pallas kernels for 0%

commit v1 on v0

v1 whole, which is shorter than its diff:
```python
import functools

import jax
import jax.numpy as jnp
from jax import lax
from jax.experimental import pallas as pl
from jax.experimental.pallas import tpu as pltpu
from jax.sharding import PartitionSpec as P

HB = 2
ITERS = 3
HALVES = 2
MESH = pl.DeviceIdType.MESH


def kernel(n_grp, n_blk, cols_ref, count_ref, pick_ref, labels_hbm, tiles_hbm, out_ref, *scratch):
    ext = scratch[0:6]
    own = scratch[6:12]
    staged = scratch[12:18]
    ext_sum = scratch[18:20]
    own_sum = scratch[20:22]
    staged_sum = scratch[22:24]
    (tiles, labels, scale, anchor_sum, coef_h, coef_l, col, load_sem, send_sem, recv_sem,
     send_sum, recv_sum) = scratch[24:]
    n_rows, kmax, bsize = tiles.shape[0], tiles.shape[1], tiles.shape[2]
    classes = labels.shape[2]
    half = classes // HALVES
    local = n_rows + 2 * HB
    zero = local + n_grp
    me = lax.axis_index("grp")
    place = lax.axis_index("blk")
    after = lax.rem(place + 1, n_blk)
    before = lax.rem(place + n_blk - 1, n_blk)

    def load(r):
        return (
            pltpu.make_async_copy(tiles_hbm.at[0, r], tiles.at[r], load_sem.at[r]),
            pltpu.make_async_copy(labels_hbm.at[0, pl.ds(r * bsize, bsize)], labels.at[r], load_sem.at[n_rows + r]),
        )

    for r in range(n_rows):
        for copy in load(r):
            copy.start()

    barrier = pltpu.get_barrier_semaphore()

    def greet(p, carry):
        pl.semaphore_signal(barrier, inc=1, device_id={"grp": lax.rem(me + p, n_grp)}, device_id_type=MESH)
        return carry

    lax.fori_loop(1, n_grp, greet, 0)
    pl.semaphore_signal(barrier, inc=1, device_id={"blk": after}, device_id_type=MESH)
    pl.semaphore_signal(barrier, inc=1, device_id={"blk": before}, device_id_type=MESH)

    def name_row(r, carry):
        used = count_ref[0, r]
        for k in range(kmax):
            c = cols_ref[0, r, k]
            block = place * n_rows + c - HB
            outside = (c < local) & ((block < 0) | (block >= n_blk * n_rows))
            col[r, k] = jnp.where((k < used) & jnp.logical_not(outside), c, zero)
        return carry

    lax.fori_loop(0, n_rows, name_row, 0)
    for ref in ext:
        ref[zero] = jnp.zeros((bsize, half), jnp.bfloat16)
    for ref in ext_sum:
        ref[zero] = jnp.zeros((1, bsize), jnp.float32)

    def keep(t, h, r, value):
        own[t * HALVES + h][r] = value
        ext[t * HALVES + h][HB + r] = value

    def keep_sum(t, r, total):
        at_row = lax.broadcasted_iota(jnp.int32, (bsize, bsize), 0)
        at_col = lax.broadcasted_iota(jnp.int32, (bsize, bsize), 1)
        spread = jnp.where(at_row == at_col, jnp.broadcast_to(total, (bsize, bsize)), 0.0)
        row = jnp.sum(spread, axis=0, keepdims=True)
        own_sum[t][r] = row
        ext_sum[t][HB + r] = row

    def halo_copies(mine, theirs, ssem, rsem, t):
        return (
            pltpu.make_async_remote_copy(
                src_ref=mine.at[pl.ds(n_rows - HB, HB)], dst_ref=theirs.at[pl.ds(0, HB)],
                send_sem=ssem.at[t, 1], recv_sem=rsem.at[t, 1], device_id={"blk": after}, device_id_type=MESH,
            ),
            pltpu.make_async_remote_copy(
                src_ref=mine.at[pl.ds(0, HB)], dst_ref=theirs.at[pl.ds(HB + n_rows, HB)],
                send_sem=ssem.at[t, 2], recv_sem=rsem.at[t, 2], device_id={"blk": before}, device_id_type=MESH,
            ),
        )

    def send(mine, out, theirs, ssem, rsem, t):
        def one(p, carry):
            other = lax.rem(me + p, n_grp)
            out[p] = mine[pick_ref[0, 0, other]]
            pltpu.make_async_remote_copy(
                src_ref=out.at[p], dst_ref=theirs.at[local + me],
                send_sem=ssem.at[t, 0], recv_sem=rsem.at[t, 0], device_id={"grp": other}, device_id_type=MESH,
            ).start()
            return carry

        lax.fori_loop(1, n_grp, one, 0)
        for copy in halo_copies(mine, theirs, ssem, rsem, t):
            copy.start()
        theirs[local + me] = mine[pick_ref[0, 0, me]]

    def wait_sent(mine, out, theirs, ssem, rsem, t):
        whole = out.at[pl.ds(1, n_grp - 1)]
        pltpu.make_async_copy(whole, whole, ssem.at[t, 0]).wait()
        for copy in halo_copies(mine, theirs, ssem, rsem, t):
            copy.wait_send()

    def wait_here(mine, theirs, ssem, rsem, t):
        whole = theirs.at[pl.ds(local, n_grp - 1)]
        pltpu.make_async_copy(whole, whole, rsem.at[t, 0]).wait()
        for copy in halo_copies(mine, theirs, ssem, rsem, t):
            copy.wait_recv()

    def field(t, h):
        i = t * HALVES + h
        return own[i], staged[i], ext[i], send_sem, recv_sem, i

    def sums(t):
        return own_sum[t], staged_sum[t], ext_sum[t], send_sum, recv_sum, t

    def arrived(of):
        wait_here(of[0], of[2], *of[3:])

    def product(t, h, r):
        blocks = ext[t * HALVES + h]
        lhs = jnp.concatenate([tiles[r, k] for k in range(kmax)], axis=1)
        rhs = jnp.concatenate([blocks[col[r, k]] for k in range(kmax)], axis=0)
        return jnp.dot(lhs, rhs, preferred_element_type=jnp.float32)

    for r in range(n_rows):
        for copy in load(r):
            copy.wait()

    def start_row(r, carry):
        total = jnp.zeros((bsize, bsize), jnp.float32)
        used = count_ref[0, r]
        for k in range(kmax):
            total += tiles[r, k].astype(jnp.float32) * jnp.where(k < used, 1.0, 0.0)
        deg = jnp.sum(total, axis=1, keepdims=True)
        factor = jnp.broadcast_to(lax.rsqrt(deg), (bsize, half))
        scale[r] = factor
        values = []
        for h in range(HALVES):
            value = (factor * labels[r, :, h * half:(h + 1) * half]).astype(jnp.bfloat16)
            keep(0, h, r, value)
            values.append(value.astype(jnp.float32))
        keep_sum(0, r, jnp.sum(values[0] + values[1], axis=1, keepdims=True))
        return carry

    lax.fori_loop(0, n_rows, start_row, 0)
    pl.semaphore_wait(barrier, n_grp + 1)
    send(*field(0, 0))
    send(*sums(0))
    send(*field(0, 1))

    def anchor_row(r, carry):
        total = jnp.sum(labels[r, :, :half] + labels[r, :, half:], axis=1, keepdims=True)
        anchor_sum[r] = jnp.broadcast_to(total, (bsize, half))
        return carry

    lax.fori_loop(0, n_rows, anchor_row, 0)

    for t in range(ITERS - 1):
        arrived(sums(t))
        arrived(field(t, 0))

        def first_row(r, carry, t=t):
            h_first = product(t, 0, r)
            total = jnp.zeros((bsize, bsize), jnp.float32)
            for k in range(kmax):
                total += tiles[r, k].astype(jnp.float32) * ext_sum[t][col[r, k]]
            total = jnp.broadcast_to(jnp.sum(total, axis=1, keepdims=True), (bsize, half))
            factor = scale[r]
            mean = (0.9 * factor * total + 0.1 * anchor_sum[r]) * (1.0 / classes)
            inverse = factor / mean
            for_h = 0.9 * factor * inverse
            for_l = 0.1 * inverse
            coef_h[r] = for_h
            coef_l[r] = for_l
            value = for_h * h_first + for_l * labels[r, :, :half]
            keep(t + 1, 0, r, value.astype(jnp.bfloat16))
            return carry

        lax.fori_loop(0, n_rows, first_row, 0)
        send(*field(t + 1, 0))
        arrived(field(t, 1))

        def second_row(r, carry, t=t):
            value = coef_h[r] * product(t, 1, r) + coef_l[r] * labels[r, :, half:]
            value = value.astype(jnp.bfloat16)
            keep(t + 1, 1, r, value)
            if t + 1 < ITERS - 1:
                both = value.astype(jnp.float32) + own[(t + 1) * HALVES][r].astype(jnp.float32)
                keep_sum(t + 1, r, jnp.sum(both, axis=1, keepdims=True))
            return carry

        lax.fori_loop(0, n_rows, second_row, 0)
        if t + 1 < ITERS - 1:
            send(*sums(t + 1))
        send(*field(t + 1, 1))

    last = ITERS - 1

    def update(h, r):
        return 0.9 * scale[r] * product(last, h, r) + 0.1 * labels[r, :, h * half:(h + 1) * half]

    arrived(field(last, 0))

    def last_first(r, carry):
        coef_h[r] = update(0, r)
        return carry

    lax.fori_loop(0, n_rows, last_first, 0)
    arrived(field(last, 1))

    def last_second(r, carry):
        second = update(1, r)
        first = coef_h[r]
        mean = jnp.sum(first + second, axis=1, keepdims=True) * (1.0 / classes)
        inverse = jnp.broadcast_to(1.0 / mean, (bsize, half))
        rows = pl.ds(pl.multiple_of(r * bsize, bsize), bsize)
        out_ref[0, rows, :half] = first * inverse
        out_ref[0, rows, half:] = second * inverse
        return carry

    lax.fori_loop(0, n_rows, last_second, 0)
    for t in range(ITERS):
        if t < ITERS - 1:
            wait_sent(*sums(t))
        for h in range(HALVES):
            wait_sent(*field(t, h))


def solution(mesh):
    n_grp, n_blk = mesh.shape["grp"], mesh.shape["blk"]

    def on_device(labels, tiles, tile_cols, tile_count, send_blocks):
        n_rows, kmax, bsize = tiles.shape[1:4]
        classes = labels.shape[2]
        half = classes // HALVES
        names = n_rows + 2 * HB + n_grp + 1
        count = ITERS * HALVES
        smem = pl.BlockSpec(memory_space=pltpu.SMEM)
        whole = pltpu.VMEM((n_rows, bsize, half), jnp.float32)
        return pl.pallas_call(
            functools.partial(kernel, n_grp, n_blk),
            name="spreading",
            out_shape=jax.ShapeDtypeStruct(labels.shape, jnp.float32),
            in_specs=[smem] * 3 + [pl.BlockSpec(memory_space=pl.ANY)] * 2,
            out_specs=pl.BlockSpec(memory_space=pltpu.VMEM),
            scratch_shapes=[pltpu.VMEM((names, bsize, half), jnp.bfloat16)] * count
            + [pltpu.VMEM((n_rows, bsize, half), jnp.bfloat16)] * count
            + [pltpu.VMEM((n_grp, bsize, half), jnp.bfloat16)] * count
            + [pltpu.VMEM((names, 1, bsize), jnp.float32)] * (ITERS - 1)
            + [pltpu.VMEM((n_rows, 1, bsize), jnp.float32)] * (ITERS - 1)
            + [pltpu.VMEM((n_grp, 1, bsize), jnp.float32)] * (ITERS - 1)
            + [
                pltpu.VMEM((n_rows, kmax, bsize, bsize), jnp.bfloat16),
                pltpu.VMEM((n_rows, bsize, classes), jnp.float32),
                whole,
                whole,
                whole,
                whole,
                pltpu.SMEM((n_rows, kmax), jnp.int32),
                pltpu.SemaphoreType.DMA((2 * n_rows,)),
                pltpu.SemaphoreType.DMA((count, 3)),
                pltpu.SemaphoreType.DMA((count, 3)),
                pltpu.SemaphoreType.DMA((ITERS - 1, 3)),
                pltpu.SemaphoreType.DMA((ITERS - 1, 3)),
            ],
            compiler_params=pltpu.CompilerParams(
                collective_id=0, has_side_effects=True, vmem_limit_bytes=60 << 20
            ),
        )(tile_cols, tile_count, send_blocks.reshape(1, 1, n_grp), labels, tiles)

    return jax.shard_map(
        on_device,
        mesh=mesh,
        in_specs=(
            P("grp", "blk", None),
            P("grp", "blk", None, None, None),
            P("grp", "blk", None),
            P("grp", "blk"),
            P("grp", "blk", None, None),
        ),
        out_specs=P("grp", "blk", None),
        check_vma=False,
    )
```

time: 263 us -> 50.9 us (0.19)
  waiting for transfers between devices: 177 us -> 0 us
  Pallas kernels: 0 us -> 48.2 us
  starting transfers between devices: 25.3 us -> 0 us
  local copies, waits for them, and re-layouts: 21.1 us -> 1.87 us
  other arithmetic: 14 us -> 0 us
  between operations: 13.3 us -> 0.01 us
  matrix products: 11.3 us -> 0 us
    all_gather x3 -> x0, waiting for transfers between devices: 164 us -> none  [on_device(): copies = lax.all_gather(own_blocks[None], 'grp', axis=0, tiled=True)]
    pallas_call x0 -> x1, Pallas kernels: none -> 48.2 us  [on_device(): pl.pallas_call(functools.partial(kernel, n_grp, n_blk), name='spreading',...]
    gather x6 -> x0, local copies, waits for them, and re-layouts: 19.6 us -> none  [the longest x3 11.3 us: on_device(): cross = copies[band_ids[:, None], arrived]]
    ppermute x6 -> x0, starting transfers between devices: 17.6 us -> none  [the longest x3 11.9 us: with_halo(): lax.ppermute(lax.slice_in_dim(block, block.shape[dim] - width, None, axis...]
    ppermute x6 -> x0, waiting for transfers between devices: 12.7 us -> none  [the longest x3 12.7 us: with_halo(): lax.ppermute(lax.slice_in_dim(block, 0, width, axis=dim), axis, backward)]
    dot_general x3 -> x0, matrix products: 11.3 us -> none  [on_device(): jnp.einsum('rkij,rkjc->ric', tiles[0], chosen, preferred_element_type=jnp...]
    all_to_all x1 -> x0, starting transfers between devices: 7.58 us -> none  [on_device(): lax.all_to_all(picks, 'grp', split_axis=0, concat_axis=0, tiled=True)]
    convert_element_type x6 -> x0, other arithmetic: 5.57 us -> none  [on_device(): scaled = (scale[:, None] * field).astype(jnp.bfloat16)]
  transfers between devices with their start and end apart: 10 -> 0, of which waited for: 6 -> 0; matrix products, arithmetic and copies ran while one was open for 1% -> 0% of each run, Pallas kernels for 0% -> 0%
where the time goes in v1:
time: 50.9 us; the launch traced here: 50.1 us
  Pallas kernels  48.2 us (95%)
  local copies, waits for them, and re-layouts  1.87 us (4%)
    pallas_call x1, Pallas kernels, on_device(): pl.pallas_call(functools.partial(kernel, n_grp, n_blk), name='spreading',...  48.2 us
    unnamed x1, local copies, waits for them, and re-layouts  1.87 us

profile of v1, /device:TPU:1, one launch (start us, length us, event | category | flops | bytes accessed | tf_op | source)
XLA Modules:
  0.0 50.1 jit_solution(17439677177917079664)
XLA Ops:
  0.0 48.2 %spreading.1 = f32[1,512,256]{2,1,0:T(8,128)} custom-call(s32[1,4,16]{2,1,0:T(4,128)} %cols_ref.1, s32[1,4]{1,0:T(1,128)} %count_ref.1, s32[1,1,16]{2,1,0:T(1,128)} %bitcast.1, f32[1,512,256]{2,1,0:T(8,128)} %labels_hbm.1, bf16[1,4,16,128,128]{4,3,2,1,0:T(8,128)(2,1)} %tiles_hbm.1), custom_call_target="tpu_custom_call" | custom-call | tf_op jit(solution)/shard_map/spreading/pallas_call | solution.py:252
  48.2 1.9 %copy.7 = f32[1,512,256]{2,1,0:T(8,128)} copy(f32[1,512,256]{2,1,0:T(8,128)} %spreading.1) | data formatting | bytes 1048576

commit v2 on v1

--- a/solution.py
+++ b/solution.py
@@ -13,14 +13,14 @@
 MESH = pl.DeviceIdType.MESH
 
 
-def kernel(n_grp, n_blk, cols_ref, count_ref, pick_ref, labels_hbm, tiles_hbm, out_ref, *scratch):
+def kernel(n_grp, n_blk, cols_hbm, count_hbm, pick_hbm, labels_hbm, tiles_hbm, out_ref, *scratch):
     ext = scratch[0:6]
     own = scratch[6:12]
     staged = scratch[12:18]
     ext_sum = scratch[18:20]
     own_sum = scratch[20:22]
     staged_sum = scratch[22:24]
-    (tiles, labels, scale, anchor_sum, coef_h, coef_l, col, load_sem, send_sem, recv_sem,
+    (tiles, labels, scale, anchor_sum, coef_h, coef_l, cols_ref, count_ref, pick_ref, col, load_sem, small_sem, send_sem, recv_sem,
      send_sum, recv_sum) = scratch[24:]
     n_rows, kmax, bsize = tiles.shape[0], tiles.shape[1], tiles.shape[2]
     classes = labels.shape[2]
@@ -38,6 +38,12 @@
             pltpu.make_async_copy(labels_hbm.at[0, pl.ds(r * bsize, bsize)], labels.at[r], load_sem.at[n_rows + r]),
         )
 
+    small = [
+        pltpu.make_async_copy(src, dst, small_sem.at[i])
+        for i, (src, dst) in enumerate(((cols_hbm, cols_ref), (count_hbm, count_ref), (pick_hbm, pick_ref)))
+    ]
+    for copy in small:
+        copy.start()
     for r in range(n_rows):
         for copy in load(r):
             copy.start()
@@ -61,6 +67,8 @@
             col[r, k] = jnp.where((k < used) & jnp.logical_not(outside), c, zero)
         return carry
 
+    for copy in small:
+        copy.wait()
     lax.fori_loop(0, n_rows, name_row, 0)
     for ref in ext:
         ref[zero] = jnp.zeros((bsize, half), jnp.bfloat16)
@@ -137,8 +145,6 @@
     for r in range(n_rows):
         for copy in load(r):
             copy.wait()
-
-    def start_row(r, carry):
         total = jnp.zeros((bsize, bsize), jnp.float32)
         used = count_ref[0, r]
         for k in range(kmax):
@@ -146,32 +152,29 @@
         deg = jnp.sum(total, axis=1, keepdims=True)
         factor = jnp.broadcast_to(lax.rsqrt(deg), (bsize, half))
         scale[r] = factor
-        values = []
-        for h in range(HALVES):
-            value = (factor * labels[r, :, h * half:(h + 1) * half]).astype(jnp.bfloat16)
-            keep(0, h, r, value)
-            values.append(value.astype(jnp.float32))
-        keep_sum(0, r, jnp.sum(values[0] + values[1], axis=1, keepdims=True))
-        return carry
-
-    lax.fori_loop(0, n_rows, start_row, 0)
+        keep(0, 0, r, (factor * labels[r, :, :half]).astype(jnp.bfloat16))
     pl.semaphore_wait(barrier, n_grp + 1)
     send(*field(0, 0))
+    for r in range(n_rows):
+        value = (scale[r] * labels[r, :, half:]).astype(jnp.bfloat16)
+        keep(0, 1, r, value)
+        both = value.astype(jnp.float32) + own[0][r].astype(jnp.float32)
+        keep_sum(0, r, jnp.sum(both, axis=1, keepdims=True))
     send(*sums(0))
     send(*field(0, 1))
 
-    def anchor_row(r, carry):
+    def anchor_row(r):
         total = jnp.sum(labels[r, :, :half] + labels[r, :, half:], axis=1, keepdims=True)
         anchor_sum[r] = jnp.broadcast_to(total, (bsize, half))
-        return carry
-
-    lax.fori_loop(0, n_rows, anchor_row, 0)
+
+    for r in range(n_rows):
+        anchor_row(r)
 
     for t in range(ITERS - 1):
         arrived(sums(t))
         arrived(field(t, 0))
 
-        def first_row(r, carry, t=t):
+        def first_row(r, t=t):
             h_first = product(t, 0, r)
             total = jnp.zeros((bsize, bsize), jnp.float32)
             for k in range(kmax):
@@ -186,22 +189,22 @@
             coef_l[r] = for_l
             value = for_h * h_first + for_l * labels[r, :, :half]
             keep(t + 1, 0, r, value.astype(jnp.bfloat16))
-            return carry
-
-        lax.fori_loop(0, n_rows, first_row, 0)
+
+        for r in range(n_rows):
+            first_row(r)
         send(*field(t + 1, 0))
         arrived(field(t, 1))
 
-        def second_row(r, carry, t=t):
+        def second_row(r, t=t):
             value = coef_h[r] * product(t, 1, r) + coef_l[r] * labels[r, :, half:]
             value = value.astype(jnp.bfloat16)
             keep(t + 1, 1, r, value)
             if t + 1 < ITERS - 1:
                 both = value.astype(jnp.float32) + own[(t + 1) * HALVES][r].astype(jnp.float32)
                 keep_sum(t + 1, r, jnp.sum(both, axis=1, keepdims=True))
-            return carry
-
-        lax.fori_loop(0, n_rows, second_row, 0)
+
+        for r in range(n_rows):
+            second_row(r)
         if t + 1 < ITERS - 1:
             send(*sums(t + 1))
         send(*field(t + 1, 1))
@@ -213,24 +216,24 @@
 
     arrived(field(last, 0))
 
-    def last_first(r, carry):
+    def last_first(r):
         coef_h[r] = update(0, r)
-        return carry
-
-    lax.fori_loop(0, n_rows, last_first, 0)
+
+    for r in range(n_rows):
+        last_first(r)
     arrived(field(last, 1))
 
-    def last_second(r, carry):
+    def last_second(r):
         second = update(1, r)
         first = coef_h[r]
         mean = jnp.sum(first + second, axis=1, keepdims=True) * (1.0 / classes)
         inverse = jnp.broadcast_to(1.0 / mean, (bsize, half))
-        rows = pl.ds(pl.multiple_of(r * bsize, bsize), bsize)
+        rows = pl.ds(r * bsize, bsize)
         out_ref[0, rows, :half] = first * inverse
         out_ref[0, rows, half:] = second * inverse
-        return carry
-
-    lax.fori_loop(0, n_rows, last_second, 0)
+
+    for r in range(n_rows):
+        last_second(r)
     for t in range(ITERS):
         if t < ITERS - 1:
             wait_sent(*sums(t))
@@ -247,13 +250,12 @@
         half = classes // HALVES
         names = n_rows + 2 * HB + n_grp + 1
         count = ITERS * HALVES
-        smem = pl.BlockSpec(memory_space=pltpu.SMEM)
         whole = pltpu.VMEM((n_rows, bsize, half), jnp.float32)
         return pl.pallas_call(
             functools.partial(kernel, n_grp, n_blk),
             name="spreading",
-            out_shape=jax.ShapeDtypeStruct(labels.shape, jnp.float32),
-            in_specs=[smem] * 3 + [pl.BlockSpec(memory_space=pl.ANY)] * 2,
+            out_shape=pltpu.VMEM(labels.shape, jnp.float32),
+            in_specs=[pl.BlockSpec(memory_space=pl.ANY)] * 5,
             out_specs=pl.BlockSpec(memory_space=pltpu.VMEM),
             scratch_shapes=[pltpu.VMEM((names, bsize, half), jnp.bfloat16)] * count
             + [pltpu.VMEM((n_rows, bsize, half), jnp.bfloat16)] * count
@@ -268,17 +270,24 @@
                 whole,
                 whole,
                 whole,
+                pltpu.SMEM((1, n_rows, kmax), jnp.int32),
+                pltpu.SMEM((1, n_rows), jnp.int32),
+                pltpu.SMEM((1, 1, n_grp), jnp.int32),
                 pltpu.SMEM((n_rows, kmax), jnp.int32),
                 pltpu.SemaphoreType.DMA((2 * n_rows,)),
+                pltpu.SemaphoreType.DMA((3,)),
                 pltpu.SemaphoreType.DMA((count, 3)),
                 pltpu.SemaphoreType.DMA((count, 3)),
                 pltpu.SemaphoreType.DMA((ITERS - 1, 3)),
                 pltpu.SemaphoreType.DMA((ITERS - 1, 3)),
             ],
             compiler_params=pltpu.CompilerParams(
-                collective_id=0, has_side_effects=True, vmem_limit_bytes=60 << 20
+                collective_id=0, has_side_effects=True, vmem_limit_bytes=32 << 20
             ),
-        )(tile_cols, tile_count, send_blocks.reshape(1, 1, n_grp), labels, tiles)
+        )(*(
+            pltpu.with_memory_space_constraint(a, pltpu.HBM)
+            for a in (tile_cols, tile_count, send_blocks.reshape(1, 1, n_grp), labels, tiles)
+        ))
 
     return jax.shard_map(
         on_device,

time: 50.9 us -> 46.3 us (0.910)
  the two profiles are of different devices: /device:TPU:1 before, /device:TPU:229 now
where the time goes in v2:
time: 46.3 us; the launch traced here: 46.1 us
  Pallas kernels  45.3 us (98%)
  local copies, waits for them, and re-layouts  0.8 us (2%)
    pallas_call x1, Pallas kernels, on_device(): pl.pallas_call(functools.partial(kernel, n_grp, n_blk), name='spreading',...  45.3 us

profile of v2, /device:TPU:229, one launch (start us, length us, event | category | flops | bytes accessed | tf_op | source)
XLA Modules:
  0.0 46.1 jit_solution(16628665045745412039)
XLA Ops:
  0.0 45.3 %spreading.1 = f32[1,512,256]{2,1,0:T(8,128)S(1)} custom-call(s32[1,4,16]{2,1,0:T(4,128)} %cols_hbm.1, s32[1,4]{1,0:T(1,128)} %count_hbm.1, s32[1,1,16]{2,1,0:T(1,128)} %bitcast.1, f32[1,512,256]{2,1,0:T(8,128)} %labels_hbm.1, bf16[1,4,16,128,128]{4,3,2,1,0:T(8,128)(2,1)} %tiles_hbm.1), custom_call_target="tpu_custom_call" | custom-call | tf_op jit(solution)/shard_map/spreading/pallas_call | solution.py:254
  45.3 0.8 %copy.7 = f32[1,512,256]{2,1,0:T(8,128)} copy(f32[1,512,256]{2,1,0:T(8,128)S(1)} %spreading.1) | data formatting | bytes 1048576

commit v3 on v2

--- a/solution.py
+++ b/solution.py
@@ -10,6 +10,10 @@
 HB = 2
 ITERS = 3
 HALVES = 2
+PIECE = 64
+ORDER = (
+    (2, 2), (0, 1), (1, 2), (3, 0), (2, 1), (0, 3), (3, 2), (1, 0), (2, 3), (1, 1), (3, 3), (0, 2), (1, 3), (3, 1), (2, 0),
+)
 MESH = pl.DeviceIdType.MESH
 
 
@@ -38,6 +42,18 @@
             pltpu.make_async_copy(labels_hbm.at[0, pl.ds(r * bsize, bsize)], labels.at[r], load_sem.at[n_rows + r]),
         )
 
+    if n_grp == 16:
+        y, x = lax.div(me, 4), lax.rem(me, 4)
+        others = [lax.rem(y + dy, 4) * 4 + lax.rem(x + dx, 4) for dy, dx in ORDER]
+    else:
+        others = [lax.rem(me + p, n_grp) for p in range(1, n_grp)]
+
+    barrier = pltpu.get_barrier_semaphore()
+    for other in others:
+        pl.semaphore_signal(barrier, inc=1, device_id={"grp": other}, device_id_type=MESH)
+    pl.semaphore_signal(barrier, inc=1, device_id={"blk": after}, device_id_type=MESH)
+    pl.semaphore_signal(barrier, inc=1, device_id={"blk": before}, device_id_type=MESH)
+
     small = [
         pltpu.make_async_copy(src, dst, small_sem.at[i])
         for i, (src, dst) in enumerate(((cols_hbm, cols_ref), (count_hbm, count_ref), (pick_hbm, pick_ref)))
@@ -47,16 +63,6 @@
     for r in range(n_rows):
         for copy in load(r):
             copy.start()
-
-    barrier = pltpu.get_barrier_semaphore()
-
-    def greet(p, carry):
-        pl.semaphore_signal(barrier, inc=1, device_id={"grp": lax.rem(me + p, n_grp)}, device_id_type=MESH)
-        return carry
-
-    lax.fori_loop(1, n_grp, greet, 0)
-    pl.semaphore_signal(barrier, inc=1, device_id={"blk": after}, device_id_type=MESH)
-    pl.semaphore_signal(barrier, inc=1, device_id={"blk": before}, device_id_type=MESH)
 
     def name_row(r, carry):
         used = count_ref[0, r]
@@ -100,22 +106,23 @@
         )
 
     def send(mine, out, theirs, ssem, rsem, t):
-        def one(p, carry):
-            other = lax.rem(me + p, n_grp)
-            out[p] = mine[pick_ref[0, 0, other]]
-            pltpu.make_async_remote_copy(
-                src_ref=out.at[p], dst_ref=theirs.at[local + me],
-                send_sem=ssem.at[t, 0], recv_sem=rsem.at[t, 0], device_id={"grp": other}, device_id_type=MESH,
-            ).start()
-            return carry
-
-        lax.fori_loop(1, n_grp, one, 0)
+        height = mine.shape[1]
+        piece = min(PIECE, height)
+        for first in range(0, height, piece):
+            rows = pl.ds(first, piece)
+            for i, other in enumerate(others):
+                if first == 0:
+                    out[i] = mine[pick_ref[0, 0, other]]
+                pltpu.make_async_remote_copy(
+                    src_ref=out.at[i, rows], dst_ref=theirs.at[local + me, rows],
+                    send_sem=ssem.at[t, 0], recv_sem=rsem.at[t, 0], device_id={"grp": other}, device_id_type=MESH,
+                ).start()
         for copy in halo_copies(mine, theirs, ssem, rsem, t):
             copy.start()
         theirs[local + me] = mine[pick_ref[0, 0, me]]
 
     def wait_sent(mine, out, theirs, ssem, rsem, t):
-        whole = out.at[pl.ds(1, n_grp - 1)]
+        whole = out.at[pl.ds(0, n_grp - 1)]
         pltpu.make_async_copy(whole, whole, ssem.at[t, 0]).wait()
         for copy in halo_copies(mine, theirs, ssem, rsem, t):
             copy.wait_send()
@@ -259,10 +266,10 @@
             out_specs=pl.BlockSpec(memory_space=pltpu.VMEM),
             scratch_shapes=[pltpu.VMEM((names, bsize, half), jnp.bfloat16)] * count
             + [pltpu.VMEM((n_rows, bsize, half), jnp.bfloat16)] * count
-            + [pltpu.VMEM((n_grp, bsize, half), jnp.bfloat16)] * count
+            + [pltpu.VMEM((n_grp - 1, bsize, half), jnp.bfloat16)] * count
             + [pltpu.VMEM((names, 1, bsize), jnp.float32)] * (ITERS - 1)
             + [pltpu.VMEM((n_rows, 1, bsize), jnp.float32)] * (ITERS - 1)
-            + [pltpu.VMEM((n_grp, 1, bsize), jnp.float32)] * (ITERS - 1)
+            + [pltpu.VMEM((n_grp - 1, 1, bsize), jnp.float32)] * (ITERS - 1)
             + [
                 pltpu.VMEM((n_rows, kmax, bsize, bsize), jnp.bfloat16),
                 pltpu.VMEM((n_rows, bsize, classes), jnp.float32),

time: 46.3 us -> 45.8 us (0.989)
  the two profiles are of different devices: /device:TPU:229 before, /device:TPU:1 now
where the time goes in v3:
time: 45.8 us; the launch traced here: 45.1 us
  Pallas kernels  44.3 us (97%)
  local copies, waits for them, and re-layouts  0.8 us (2%)
    pallas_call x1, Pallas kernels, on_device(): pl.pallas_call(functools.partial(kernel, n_grp, n_blk), name='spreading',...  44.3 us

profile of v3, /device:TPU:1, one launch (start us, length us, event | category | flops | bytes accessed | tf_op | source)
XLA Modules:
  0.0 45.1 jit_solution(6909724292435740094)
XLA Ops:
  0.0 44.3 %spreading.1 = f32[1,512,256]{2,1,0:T(8,128)S(1)} custom-call(s32[1,4,16]{2,1,0:T(4,128)} %cols_hbm.1, s32[1,4]{1,0:T(1,128)} %count_hbm.1, s32[1,1,16]{2,1,0:T(1,128)} %bitcast.1, f32[1,512,256]{2,1,0:T(8,128)} %labels_hbm.1, bf16[1,4,16,128,128]{4,3,2,1,0:T(8,128)(2,1)} %tiles_hbm.1), custom_call_target="tpu_custom_call" | custom-call | tf_op jit(solution)/shard_map/spreading/pallas_call | solution.py:261
  44.4 0.8 %copy.7 = f32[1,512,256]{2,1,0:T(8,128)} copy(f32[1,512,256]{2,1,0:T(8,128)S(1)} %spreading.1) | data formatting | bytes 1048576

commit v4 on v3

--- a/solution.py
+++ b/solution.py
@@ -42,18 +42,6 @@
             pltpu.make_async_copy(labels_hbm.at[0, pl.ds(r * bsize, bsize)], labels.at[r], load_sem.at[n_rows + r]),
         )
 
-    if n_grp == 16:
-        y, x = lax.div(me, 4), lax.rem(me, 4)
-        others = [lax.rem(y + dy, 4) * 4 + lax.rem(x + dx, 4) for dy, dx in ORDER]
-    else:
-        others = [lax.rem(me + p, n_grp) for p in range(1, n_grp)]
-
-    barrier = pltpu.get_barrier_semaphore()
-    for other in others:
-        pl.semaphore_signal(barrier, inc=1, device_id={"grp": other}, device_id_type=MESH)
-    pl.semaphore_signal(barrier, inc=1, device_id={"blk": after}, device_id_type=MESH)
-    pl.semaphore_signal(barrier, inc=1, device_id={"blk": before}, device_id_type=MESH)
-
     small = [
         pltpu.make_async_copy(src, dst, small_sem.at[i])
         for i, (src, dst) in enumerate(((cols_hbm, cols_ref), (count_hbm, count_ref), (pick_hbm, pick_ref)))
@@ -63,6 +51,18 @@
     for r in range(n_rows):
         for copy in load(r):
             copy.start()
+
+    if n_grp == 16:
+        y, x = lax.div(me, 4), lax.rem(me, 4)
+        others = [lax.rem(y + dy, 4) * 4 + lax.rem(x + dx, 4) for dy, dx in ORDER]
+    else:
+        others = [lax.rem(me + p, n_grp) for p in range(1, n_grp)]
+
+    barrier = pltpu.get_barrier_semaphore()
+    for other in others:
+        pl.semaphore_signal(barrier, inc=1, device_id={"grp": other}, device_id_type=MESH)
+    pl.semaphore_signal(barrier, inc=1, device_id={"blk": after}, device_id_type=MESH)
+    pl.semaphore_signal(barrier, inc=1, device_id={"blk": before}, device_id_type=MESH)
 
     def name_row(r, carry):
         used = count_ref[0, r]

time: 45.8 us -> 45.8 us (level)
  no operation moved by 1% of the time
where the time goes in v4:
time: 45.8 us; the launch traced here: 45.1 us
  Pallas kernels  44.3 us (97%)
  local copies, waits for them, and re-layouts  0.8 us (2%)
    pallas_call x1, Pallas kernels, on_device(): pl.pallas_call(functools.partial(kernel, n_grp, n_blk), name='spreading',...  44.3 us

profile of v4, /device:TPU:1, one launch (start us, length us, event | category | flops | bytes accessed | tf_op | source)
XLA Modules:
  0.0 45.1 jit_solution(3115584113247782704)
XLA Ops:
  0.0 44.3 %spreading.1 = f32[1,512,256]{2,1,0:T(8,128)S(1)} custom-call(s32[1,4,16]{2,1,0:T(4,128)} %cols_hbm.1, s32[1,4]{1,0:T(1,128)} %count_hbm.1, s32[1,1,16]{2,1,0:T(1,128)} %bitcast.1, f32[1,512,256]{2,1,0:T(8,128)} %labels_hbm.1, bf16[1,4,16,128,128]{4,3,2,1,0:T(8,128)(2,1)} %tiles_hbm.1), custom_call_target="tpu_custom_call" | custom-call | tf_op jit(solution)/shard_map/spreading/pallas_call | solution.py:261
  44.3 0.8 %copy.7 = f32[1,512,256]{2,1,0:T(8,128)} copy(f32[1,512,256]{2,1,0:T(8,128)S(1)} %spreading.1) | data formatting | bytes 1048576

commit v5 on v3

--- a/solution.py
+++ b/solution.py
@@ -154,10 +154,16 @@
             copy.wait()
         total = jnp.zeros((bsize, bsize), jnp.float32)
         used = count_ref[0, r]
-        for k in range(kmax):
+        for k in range(kmax // 2):
             total += tiles[r, k].astype(jnp.float32) * jnp.where(k < used, 1.0, 0.0)
-        deg = jnp.sum(total, axis=1, keepdims=True)
-        factor = jnp.broadcast_to(lax.rsqrt(deg), (bsize, half))
+        later = range(kmax // 2, kmax)
+        ones = [jnp.broadcast_to(jnp.where(k < used, 1.0, 0.0), (bsize, half)).astype(jnp.bfloat16) for k in later]
+        deg = jnp.sum(total, axis=1, keepdims=True) + jnp.dot(
+            jnp.concatenate([tiles[r, k] for k in later], axis=1),
+            jnp.concatenate(ones, axis=0),
+            preferred_element_type=jnp.float32,
+        )
+        factor = lax.rsqrt(deg)
         scale[r] = factor
         keep(0, 0, r, (factor * labels[r, :, :half]).astype(jnp.bfloat16))
     pl.semaphore_wait(barrier, n_grp + 1)

time: 45.8 us -> 45.8 us (level)
  no operation moved by 1% of the time
where the time goes in v5:
time: 45.8 us; the launch traced here: 45.1 us
  Pallas kernels  44.3 us (97%)
  local copies, waits for them, and re-layouts  0.8 us (2%)
    pallas_call x1, Pallas kernels, on_device(): pl.pallas_call(functools.partial(kernel, n_grp, n_blk), name='spreading',...  44.3 us

profile of v5, /device:TPU:1, one launch (start us, length us, event | category | flops | bytes accessed | tf_op | source)
XLA Modules:
  0.0 45.1 jit_solution(17732046084031734830)
XLA Ops:
  0.0 44.3 %spreading.1 = f32[1,512,256]{2,1,0:T(8,128)S(1)} custom-call(s32[1,4,16]{2,1,0:T(4,128)} %cols_hbm.1, s32[1,4]{1,0:T(1,128)} %count_hbm.1, s32[1,1,16]{2,1,0:T(1,128)} %bitcast.1, f32[1,512,256]{2,1,0:T(8,128)} %labels_hbm.1, bf16[1,4,16,128,128]{4,3,2,1,0:T(8,128)(2,1)} %tiles_hbm.1), custom_call_target="tpu_custom_call" | custom-call | tf_op jit(solution)/shard_map/spreading/pallas_call | solution.py:267
  44.3 0.8 %copy.7 = f32[1,512,256]{2,1,0:T(8,128)} copy(f32[1,512,256]{2,1,0:T(8,128)S(1)} %spreading.1) | data formatting | bytes 1048576

commit v6 on v5

--- a/solution.py
+++ b/solution.py
@@ -105,13 +105,17 @@
             ),
         )
 
-    def send(mine, out, theirs, ssem, rsem, t):
+    def pick(mine, out):
+        for i, other in enumerate(others):
+            out[i] = mine[pick_ref[0, 0, other]]
+
+    def send(mine, out, theirs, ssem, rsem, t, picked=False):
         height = mine.shape[1]
         piece = min(PIECE, height)
         for first in range(0, height, piece):
             rows = pl.ds(first, piece)
             for i, other in enumerate(others):
-                if first == 0:
+                if first == 0 and not picked:
                     out[i] = mine[pick_ref[0, 0, other]]
                 pltpu.make_async_remote_copy(
                     src_ref=out.at[i, rows], dst_ref=theirs.at[local + me, rows],
@@ -166,8 +170,9 @@
         factor = lax.rsqrt(deg)
         scale[r] = factor
         keep(0, 0, r, (factor * labels[r, :, :half]).astype(jnp.bfloat16))
+    pick(*field(0, 0)[:2])
     pl.semaphore_wait(barrier, n_grp + 1)
-    send(*field(0, 0))
+    send(*field(0, 0), picked=True)
     for r in range(n_rows):
         value = (scale[r] * labels[r, :, half:]).astype(jnp.bfloat16)
         keep(0, 1, r, value)

time: 45.8 us -> 45.8 us (level)
  no operation moved by 1% of the time
where the time goes in v6:
time: 45.8 us; the launch traced here: 45.2 us
  Pallas kernels  44.4 us (97%)
  local copies, waits for them, and re-layouts  0.8 us (2%)
    pallas_call x1, Pallas kernels, on_device(): pl.pallas_call(functools.partial(kernel, n_grp, n_blk), name='spreading',...  44.4 us

profile of v6, /device:TPU:1, one launch (start us, length us, event | category | flops | bytes accessed | tf_op | source)
XLA Modules:
  0.0 45.2 jit_solution(4015782317625732336)
XLA Ops:
  0.0 44.4 %spreading.1 = f32[1,512,256]{2,1,0:T(8,128)S(1)} custom-call(s32[1,4,16]{2,1,0:T(4,128)} %cols_hbm.1, s32[1,4]{1,0:T(1,128)} %count_hbm.1, s32[1,1,16]{2,1,0:T(1,128)} %bitcast.1, f32[1,512,256]{2,1,0:T(8,128)} %labels_hbm.1, bf16[1,4,16,128,128]{4,3,2,1,0:T(8,128)(2,1)} %tiles_hbm.1), custom_call_target="tpu_custom_call" | custom-call | tf_op jit(solution)/shard_map/spreading/pallas_call | solution.py:272
  44.5 0.8 %copy.7 = f32[1,512,256]{2,1,0:T(8,128)} copy(f32[1,512,256]{2,1,0:T(8,128)S(1)} %spreading.1) | data formatting | bytes 1048576
